TPU v7x, 32 devices: a whole 2x2x4 slice. The times are simulated.
32 devices in a mesh: seq: 16 (over z, y, x), chan: 2 (over core).
Axes of the slice: x: 2, y: 2, z: 4, core: 2. Of those that a mesh axis runs over, the one named last changes fastest.
Arguments:
- projected: bfloat16 [2048, 3, 4096], P('seq', None, 'chan'), may hold values from -6 to 6
- short_weight: float32 [3, 3, 4096], P(None, None, 'chan'), may hold values from -3 to 3
- filter_taps: float32 [2048, 4096], P('seq', 'chan'), may hold values from -1 to 1, as said below
- skip_gain: float32 [4096], P('chan'), may hold values from -4 to 4
- stream: bfloat16 [2048, 4096], P('seq', 'chan'), may hold values from -6 to 6
- norm_gain: float32 [4096], P('chan'), may hold values from 0.5 to 1.5
Outputs:
- mixed: bfloat16 [2048, 4096], P('seq', 'chan')
- normed: bfloat16 [2048, 4096], P('seq', 'chan')
Inputs may be any that keep to these rules, and one draw needn't show every extreme that they name: `filter_taps`: taps of a causal filter.
All inputs are finite; a program needn't handle non-finite values.
Results may differ from a plain program's by a relative error of at most 0.001.
Values may be sent and summed in bfloat16 or wider, within the bound.
A program may use at most 64 MiB of HBM per device.

v0:
```python
import functools
import math

import jax
import jax.numpy as jnp
import ml_dtypes
import numpy as np
from jax import lax
from jax.experimental import pallas as pl
from jax.experimental.pallas import tpu as pltpu
from jax.sharding import PartitionSpec as P

D = 4096


high = lax.Precision.HIGHEST


def shifted(x, axis, by):
    count = lax.axis_size(axis)
    pairs = [(i, i + by) for i in range(count) if 0 <= i + by < count]
    return lax.ppermute(x, axis, pairs)


def tables(rows, cols, length):
    product = rows[:, None] * cols[None, :] % length
    angle = 2.0 * math.pi / length * product.astype(jnp.float32)
    return (jnp.cos(angle), jnp.sin(angle))


def local_convolve(signals, groups, rows):
    total = 2 * groups * rows
    chans = signals.shape[1]
    blocks_io = jnp.arange(groups, dtype=jnp.int32)
    freq_io = jnp.arange(2 * groups, dtype=jnp.int32)
    pos_io = jnp.arange(rows, dtype=jnp.int32)
    cos_outer, sin_outer = tables(freq_io, blocks_io, 2 * groups)
    cos_twist, sin_twist = tables(freq_io, pos_io, total)
    cos_inner, sin_inner = tables(pos_io, pos_io, rows)
    shaped = signals.reshape(2, chans, groups, rows)
    outer_re = jnp.einsum("ka,wcab->wckb", cos_outer, shaped, precision=high)
    outer_im = -jnp.einsum("ka,wcab->wckb", sin_outer, shaped, precision=high)
    turn_re = outer_re * cos_twist + outer_im * sin_twist
    turn_im = outer_im * cos_twist - outer_re * sin_twist
    spec_re = jnp.einsum("wckb,bf->wckf", turn_re, cos_inner, precision=high) + jnp.einsum(
        "wckb,bf->wckf", turn_im, sin_inner, precision=high
    )
    spec_im = jnp.einsum("wckb,bf->wckf", turn_im, cos_inner, precision=high) - jnp.einsum(
        "wckb,bf->wckf", turn_re, sin_inner, precision=high
    )
    prod_re = spec_re[0] * spec_re[1] - spec_im[0] * spec_im[1]
    prod_im = spec_re[0] * spec_im[1] + spec_im[0] * spec_re[1]
    inner_re = jnp.einsum("ckf,fb->ckb", prod_re, cos_inner, precision=high) - jnp.einsum(
        "ckf,fb->ckb", prod_im, sin_inner, precision=high
    )
    inner_im = jnp.einsum("ckf,fb->ckb", prod_im, cos_inner, precision=high) + jnp.einsum(
        "ckf,fb->ckb", prod_re, sin_inner, precision=high
    )
    back_re = inner_re * cos_twist - inner_im * sin_twist
    back_im = inner_im * cos_twist + inner_re * sin_twist
    cos_final, sin_final = tables(blocks_io, freq_io, 2 * groups)
    result = jnp.einsum("ak,ckb->cab", cos_final, back_re, precision=high) - jnp.einsum(
        "ak,ckb->cab", sin_final, back_im, precision=high
    )
    return (result / total).reshape(chans, groups * rows)


def shards(projected, short_weight, filter_taps, skip_gain, stream, norm_gain):
    rows = projected.shape[0]
    groups = lax.axis_size("seq")
    previous = shifted(projected[rows - 2 :], "seq", 1)
    ext = jnp.concatenate([previous, projected], axis=0).astype(jnp.float32)
    featured = short_weight[0] * ext[2:] + short_weight[1] * ext[1:-1] + short_weight[2] * ext[:-2]
    x_one = featured[:, 0]
    gated = featured[:, 1] * featured[:, 2]
    whole = lax.all_to_all(
        jnp.stack([gated, filter_taps]), "seq", split_axis=2, concat_axis=1, tiled=True
    )
    signals = jnp.transpose(whole, (0, 2, 1))
    convolved = local_convolve(signals, groups, rows)
    conv = lax.all_to_all(convolved.T, "seq", split_axis=0, concat_axis=1, tiled=True)
    mixer = (conv + skip_gain * gated) * x_one
    mixed = mixer.astype(jnp.bfloat16)
    summed = stream.astype(jnp.float32) + mixer
    power = lax.psum(jnp.sum(summed * summed, axis=1), "chan")
    normed = (summed / jnp.sqrt(power[:, None] / D + 1e-05) * norm_gain).astype(jnp.bfloat16)
    return (mixed, normed)


MESH = pl.DeviceIdType.MESH
POWER = 16
TOP = 2.0**7.75


def encode(x):
    most = jnp.maximum(jnp.max(jnp.abs(x), axis=0, keepdims=True), 1e-30)
    r = x * (TOP / most)
    p = r * r
    p = p * p
    p = p * p
    p = p * p
    return jnp.where(r < 0.0, -p, p).astype(jnp.bfloat16), most * (1.0 / TOP)


def decode(code, scale):
    y = code.astype(jnp.float32)
    mag = jnp.abs(y)
    root = jnp.exp(jnp.log(jnp.maximum(mag, 1e-38)) * (1.0 / POWER)) * scale
    root = jnp.where(mag > 0.0, root, 0.0)
    return jnp.where(y < 0.0, -root, root)


def split3(x):
    hi = x.astype(jnp.bfloat16)
    lo = (x - hi.astype(jnp.float32)).astype(jnp.bfloat16)
    return jnp.concatenate([hi, lo, hi], axis=0)


def dot(a, b):
    return jnp.dot(a, b, preferred_element_type=jnp.float32)


def wide(mat):
    hi = mat.astype(ml_dtypes.bfloat16)
    lo = (mat - hi.astype(np.float64)).astype(ml_dtypes.bfloat16)
    return np.concatenate([hi, hi, lo], axis=1)


def constants(groups, rows, fine):
    total = 2 * groups * rows
    ks = groups + 2
    k = np.arange(ks)
    a = np.arange(groups)
    b = np.arange(rows)
    live = (k <= groups).astype(np.float64)
    angle = 2.0 * np.pi * (k[:, None] * a[None, :] % (2 * groups)) / (2 * groups)
    eye = np.eye(fine)
    fwd = np.stack([np.cos(angle), -np.sin(angle)], axis=1) * live[:, None, None]
    outer = np.einsum("kra,xy->krxay", fwd, eye).reshape(ks * 2 * fine, groups * fine)
    weight = np.where((k == 0) | (k == groups), 1.0, 2.0) * live / total
    back = np.einsum("kra,xy->axkry", fwd * weight[:, None, None], eye)
    back = back.reshape(groups * fine, ks * 2 * fine)
    inner = 2.0 * np.pi * (b[:, None] * b[None, :] % rows) / rows
    c, s = np.cos(inner), np.sin(inner)
    mat = np.block([[c, s], [-s, c]])
    turn = 2.0 * np.pi * (k[:, None] * b[None, :] % total) / total
    spread = np.stack([np.cos(turn), np.sin(turn)], axis=1)[..., None]
    spread = np.broadcast_to(spread, (ks, 2, rows, 128)).astype(np.float32)
    return wide(outer), wide(mat), wide(mat.T), wide(back), spread


def outer_forward(n, rows, outer, x, y):
    ks = n + 2

    def step(j, carry):
        parts = []
        for half in range(2):
            at = pl.ds(pl.multiple_of(j * 32 + 16 * half, 16), 16)
            parts.append(x[:, at, :].reshape(n * 16, 128))
        u = dot(outer[...], split3(jnp.concatenate(parts, axis=1)))
        for half in range(2):
            at = pl.ds(pl.multiple_of(j * 32 + 16 * half, 16), 16)
            y[:, :, at, :] = u[:, 128 * half : 128 * half + 128].reshape(ks, 2, 16, 128)
        return carry

    lax.fori_loop(0, rows // 32, step, 0)


def inner_forward(pair, rows, inner, turn, y):
    parts = []
    for half in range(2):
        k = 2 * pair + half
        re, im, c, s = y[k, 0], y[k, 1], turn[k, 0], turn[k, 1]
        parts.append(jnp.concatenate([re * c + im * s, im * c - re * s], axis=0))
    return dot(inner[...], split3(jnp.concatenate(parts, axis=1)))


def kernel(
    n, x_hbm, w_hbm, taps_hbm, skip_hbm, stream_hbm, gain_hbm, outer_hbm, inner_hbm, inner_back_hbm,
    back_hbm, turn_hbm, mixed_ref, normed_ref,
    x_ref, w_ref, taps_ref, skip_ref, stream_ref, gain_ref, outer, inner, inner_back, back, turn,
    gated_ref, one_ref, tail, halo, hsend, hsscale, hcode, hscale, gsend, gsscale, gcode, gscale,
    csend, csscale, ccode, cscale, x, y, z, summed, mine, other, sems, edge_sems, local_sems,
):
    me = lax.axis_index("seq")
    core = lax.axis_index("chan")
    rows = x_ref.shape[1]
    part = rows // 2
    barrier = pltpu.get_barrier_semaphore()

    def greet(o, carry):
        pl.semaphore_signal(
            barrier, inc=1, device_id={"seq": lax.rem(me + o, n)}, device_id_type=MESH
        )
        return carry

    lax.fori_loop(1, n, greet, 0)
    pl.semaphore_signal(barrier, inc=1, device_id={"chan": 1 - core}, device_id_type=MESH)

    moves = [(x_hbm, x_ref), (taps_hbm, taps_ref), (w_hbm, w_ref), (outer_hbm, outer),
             (turn_hbm, turn), (inner_hbm, inner), (inner_back_hbm, inner_back), (back_hbm, back),
             (stream_hbm, stream_ref), (skip_hbm, skip_ref), (gain_hbm, gain_ref)]
    loads = []
    for i, (src, dst) in enumerate(moves):
        load = pltpu.make_async_copy(src, dst, local_sems.at[i])
        load.start()
        loads.append(load)

    def lanes(d):
        return pl.ds(pl.multiple_of(d * 128, 128), 128)

    def link(kind, o, src, dst):
        return pltpu.make_async_remote_copy(
            src_ref=src,
            dst_ref=dst,
            send_sem=sems.at[2 * kind, o],
            recv_sem=sems.at[2 * kind + 1, o],
            device_id={"seq": lax.rem(me + o, n)},
            device_id_type=MESH,
        )

    def taps_links(o):
        to = lax.rem(me + o, n)
        return (link(0, o, hsend.at[to], hcode.at[me]), link(1, o, hsscale.at[to], hscale.at[me]))

    def gated_links(o):
        to = lax.rem(me + o, n)
        return (link(2, o, gsend.at[to], gcode.at[me]), link(3, o, gsscale.at[to], gscale.at[me]))

    def conv_links(p, o):
        to = lax.rem(me + o, n)
        at = pl.ds(p * part, part)
        return (
            link(4 + 2 * p, o, csend.at[to, at], ccode.at[me, at]),
            link(5 + 2 * p, o, csscale.at[p, to], cscale.at[p, me]),
        )

    loads[0].wait()
    for j in range(3):
        last = x_ref[j, rows - 16 :, :].astype(jnp.float32)
        tail[2 * j : 2 * j + 2, :] = last[14:16, :]
    loads[1].wait()
    pl.semaphore_wait(barrier, n)
    after = pltpu.make_async_remote_copy(
        src_ref=tail,
        dst_ref=halo,
        send_sem=edge_sems.at[0],
        recv_sem=edge_sems.at[1],
        device_id={"seq": lax.rem(me + 1, n)},
        device_id_type=MESH,
    )
    after.start()

    def send_taps(o, carry):
        to = lax.rem(me + o, n)
        hsend[to], hsscale[to] = encode(taps_ref[:, lanes(to)])
        for copy in taps_links(o):
            copy.start()
        return carry

    lax.fori_loop(1, n, send_taps, 0)
    x[me] = taps_ref[:, lanes(me)]
    loads[2].wait()
    after.wait()
    first = jnp.where(me > 0, 1.0, 0.0).astype(jnp.float32)

    def feature(d):
        cols = lanes(d)
        prev = halo[:, cols] * first
        feats = []
        for j in range(3):
            now = x_ref[j, :, cols].astype(jnp.float32)
            ext = jnp.concatenate([prev[2 * j : 2 * j + 2], now], axis=0)
            feats.append(
                w_ref[0, j : j + 1, cols] * now
                + w_ref[1, j : j + 1, cols] * ext[1 : rows + 1]
                + w_ref[2, j : j + 1, cols] * ext[:rows]
            )
        gated = feats[1] * feats[2]
        one_ref[:, cols] = feats[0]
        gated_ref[:, cols] = gated
        return gated

    def send_gated(o, carry):
        to = lax.rem(me + o, n)
        gsend[to], gsscale[to] = encode(feature(to))
        for copy in gated_links(o):
            copy.start()
        return carry

    lax.fori_loop(1, n, send_gated, 0)
    feature(me)

    def take_taps(o, carry):
        source = lax.rem(me - o + n, n)
        for copy in taps_links(o):
            copy.wait()
        x[source] = decode(hcode[source], hscale[source])
        return carry

    lax.fori_loop(1, n, take_taps, 0)
    for load in loads[3:8]:
        load.wait()
    outer_forward(n, rows, outer, x, y)

    def spectrum(pair, carry):
        z[pair] = inner_forward(pair, rows, inner, turn, y)
        return carry

    lax.fori_loop(0, (n + 2) // 2, spectrum, 0)
    x[me] = gated_ref[:, lanes(me)]

    def take_gated(o, carry):
        source = lax.rem(me - o + n, n)
        for copy in gated_links(o):
            copy.wait()
        x[source] = decode(gcode[source], gscale[source])
        return carry

    lax.fori_loop(1, n, take_gated, 0)
    outer_forward(n, rows, outer, x, y)

    def multiply(pair, carry):
        g = inner_forward(pair, rows, inner, turn, y)
        h = z[pair]
        gr, gi, hr, hi = g[:rows], g[rows:], h[:rows], h[rows:]
        prod = jnp.concatenate([gr * hr - gi * hi, gr * hi + gi * hr], axis=0)
        v = dot(inner_back[...], split3(prod))
        for half in range(2):
            k = 2 * pair + half
            side = slice(128 * half, 128 * half + 128)
            re, im, c, s = v[:rows, side], v[rows:, side], turn[k, 0], turn[k, 1]
            y[k, 0] = re * c - im * s
            y[k, 1] = im * c + re * s
        return carry

    lax.fori_loop(0, (n + 2) // 2, multiply, 0)

    def blocks(j, carry):
        parts = []
        for half in range(2):
            at = pl.ds(pl.multiple_of(j * 32 + 16 * half, 16), 16)
            parts.append(y[:, :, at, :].reshape((n + 2) * 32, 128))
        u = dot(back[...], split3(jnp.concatenate(parts, axis=1)))
        for half in range(2):
            at = pl.ds(pl.multiple_of(j * 32 + 16 * half, 16), 16)
            x[:, at, :] = u[:, 128 * half : 128 * half + 128].reshape(n, 16, 128)
        return carry

    for p in range(2):
        lax.fori_loop(p * part // 32, (p + 1) * part // 32, blocks, 0)

        def send_conv(o, carry, p=p):
            to = lax.rem(me + o, n)
            at = pl.ds(p * part, part)
            csend[to, at, :], csscale[p, to] = encode(x[to, at, :])
            for copy in conv_links(p, o):
                copy.start()
            return carry

        lax.fori_loop(1, n, send_conv, 0)

    for load in loads[8:]:
        load.wait()
    mine[...] = jnp.zeros_like(mine)

    def mix(p, d, conv):
        at, cols = pl.ds(p * part, part), lanes(d)
        mixer = (conv + skip_ref[:, cols] * gated_ref[at, cols]) * one_ref[at, cols]
        mixed_ref[at, cols] = mixer.astype(jnp.bfloat16)
        both = stream_ref[at, cols].astype(jnp.float32) + mixer
        summed[at, cols] = both
        mine[at, :] += both * both

    for p in range(2):
        mix(p, me, x[me, pl.ds(p * part, part), :])

        def take_conv(o, carry, p=p):
            source = lax.rem(me - o + n, n)
            for copy in conv_links(p, o):
                copy.wait()
            mix(p, source, decode(ccode[source, pl.ds(p * part, part), :], cscale[p, source]))
            return carry

        lax.fori_loop(1, n, take_conv, 0)

    swap = pltpu.make_async_remote_copy(
        src_ref=mine,
        dst_ref=other,
        send_sem=edge_sems.at[2],
        recv_sem=edge_sems.at[3],
        device_id={"chan": 1 - core},
        device_id_type=MESH,
    )
    swap.start()
    swap.wait()
    power = jnp.sum(mine[...] + other[...], axis=1, keepdims=True)
    factor = 1.0 / jnp.sqrt(power / D + 1e-05)

    def norm(d, carry):
        cols = lanes(d)
        normed_ref[:, cols] = (summed[:, cols] * factor * gain_ref[:, cols]).astype(jnp.bfloat16)
        return carry

    lax.fori_loop(0, n, norm, 0)


def fast(n, projected, short_weight, filter_taps, skip_gain, stream, norm_gain):
    rows, _, chans = projected.shape
    f32, bf16 = jnp.float32, jnp.bfloat16
    codes, scales, ks = (n, rows, 128), (n, 1, 128), n + 2
    operands = [
        jnp.transpose(projected, (1, 0, 2)), short_weight, filter_taps,
        skip_gain.reshape(1, chans), stream, norm_gain.reshape(1, chans),
    ] + [jnp.asarray(table) for table in constants(n, rows, 16)]
    pair = [pltpu.VMEM(codes, bf16), pltpu.VMEM(scales, f32)]
    return pl.pallas_call(
        functools.partial(kernel, n),
        out_shape=[jax.ShapeDtypeStruct((rows, chans), bf16)] * 2,
        in_specs=[pl.BlockSpec(memory_space=pl.ANY)] * len(operands),
        out_specs=[pl.BlockSpec(memory_space=pltpu.VMEM)] * 2,
        scratch_shapes=[pltpu.VMEM(array.shape, array.dtype) for array in operands]
        + [pltpu.VMEM((rows, chans), f32)] * 2
        + [pltpu.VMEM((8, chans), f32)] * 2
        + pair * 4
        + [pltpu.VMEM(codes, bf16), pltpu.VMEM((2,) + scales, f32)] * 2
        + [
            pltpu.VMEM(codes, f32),
            pltpu.VMEM((ks, 2, rows, 128), f32),
            pltpu.VMEM((ks // 2, 2 * rows, 256), f32),
            pltpu.VMEM((rows, chans), f32),
            pltpu.VMEM((rows, 128), f32),
            pltpu.VMEM((rows, 128), f32),
            pltpu.SemaphoreType.DMA((16, n)),
            pltpu.SemaphoreType.DMA((4,)),
            pltpu.SemaphoreType.DMA((len(operands),)),
        ],
        compiler_params=pltpu.CompilerParams(
            collective_id=0, has_side_effects=True, vmem_limit_bytes=56 * 2**20
        ),
        name="mixer",
    )(*operands)


def solution(mesh):
    n, cores = mesh.shape["seq"], mesh.shape["chan"]

    def local(*args):
        rows, _, chans = args[0].shape
        if cores == 2 and chans == 128 * n and rows == 128 and n % 2 == 0:
            return tuple(fast(n, *args))
        return shards(*args)

    in_specs = (
        P("seq", None, "chan"),
        P(None, None, "chan"),
        P("seq", "chan"),
        P("chan"),
        P("seq", "chan"),
        P("chan"),
    )
    out_specs = (P("seq", "chan"), P("seq", "chan"))
    return jax.shard_map(local, mesh=mesh, in_specs=in_specs, out_specs=out_specs, check_vma=False)
```

profile of v0, /device:TPU:0, one launch (start us, length us, event | category | flops | bytes accessed | tf_op | source)
XLA Modules:
  0.0 62.2 jit_solution(2060600721927707656)
XLA Ops:
  0.6 57.8 %mixer.1 = (bf16[128,2048]{1,0:T(8,128)(2,1)}, bf16[128,2048]{1,0:T(8,128)(2,1)}) custom-call(bf16[3,128,2048]{2,1,0:T(8,128)(2,1)} %bitcast.3, f32[3,3,2048]{2,1,0:T(4,128)} %w_hbm.1, f32[128,2048]{1,0:T(8,128)} %taps_hbm.1, f32[1,2048]{1,0:T(1,128)} %bitcast.4, bf16[128,2048]{1,0:T(8,128)(2,1)} %stream_hbm.1, f32[1,2048]{1,0:T(1,128)} %bitcast.5, ...), custom_call_target="tpu_custom_call" | custom-call | tf_op jit(solution)/shard_map/mixer/pallas_call | solution.py:417
  58.4 1.9 %copy.15 = bf16[128,2048]{1,0:T(8,128)(2,1)} copy(bf16[128,2048]{1,0:T(8,128)(2,1)} %get-tuple-element.4) | data formatting | bytes 1048576
  60.3 1.9 %copy.16 = bf16[128,2048]{1,0:T(8,128)(2,1)} copy(bf16[128,2048]{1,0:T(8,128)(2,1)} %get-tuple-element.5) | data formatting | bytes 1048576
where the time goes:
time: 62.4 us; the launch traced here: 62.2 us
  Pallas kernels  57.8 us (93%)
  local copies, waits for them, and re-layouts  3.76 us (6%)
  between operations  0.64 us (1%)
    pallas_call x1, Pallas kernels, fast(): pl.pallas_call(functools.partial(kernel, n), out_shape=[jax.ShapeDtypeStr...  57.8 us
    unnamed x2, local copies, waits for them, and re-layouts  3.76 us

commit v1 on v0

--- a/solution.py
+++ b/solution.py
@@ -149,7 +149,7 @@
     return wide(outer), wide(mat), wide(mat.T), wide(back), spread
 
 
-def outer_forward(n, rows, outer, x, y):
+def outer_forward(n, begin, end, outer, x, y):
     ks = n + 2
 
     def step(j, carry):
@@ -163,7 +163,7 @@
             y[:, :, at, :] = u[:, 128 * half : 128 * half + 128].reshape(ks, 2, 16, 128)
         return carry
 
-    lax.fori_loop(0, rows // 32, step, 0)
+    lax.fori_loop(begin // 32, end // 32, step, 0)
 
 
 def inner_forward(pair, rows, inner, turn, y):
@@ -185,7 +185,8 @@
     me = lax.axis_index("seq")
     core = lax.axis_index("chan")
     rows = x_ref.shape[1]
-    part = rows // 2
+    half_rows = rows // 2
+    spans = ((0, rows // 4), (rows // 4, rows))
     barrier = pltpu.get_barrier_semaphore()
 
     def greet(o, carry):
@@ -225,21 +226,33 @@
 
     def gated_links(o):
         to = lax.rem(me + o, n)
-        return (link(2, o, gsend.at[to], gcode.at[me]), link(3, o, gsscale.at[to], gscale.at[me]))
+        low, high = pl.ds(0, half_rows), pl.ds(half_rows, half_rows)
+        return (
+            link(2, o, gsend.at[to, low], gcode.at[me, low]),
+            link(3, o, gsscale.at[to], gscale.at[me]),
+            link(4, o, gsend.at[to, high], gcode.at[me, high]),
+        )
 
     def conv_links(p, o):
         to = lax.rem(me + o, n)
-        at = pl.ds(p * part, part)
+        at = pl.ds(spans[p][0], spans[p][1] - spans[p][0])
         return (
-            link(4 + 2 * p, o, csend.at[to, at], ccode.at[me, at]),
-            link(5 + 2 * p, o, csscale.at[p, to], cscale.at[p, me]),
+            link(5 + 2 * p, o, csend.at[to, at], ccode.at[me, at]),
+            link(6 + 2 * p, o, csscale.at[p, to], cscale.at[p, me]),
         )
 
+    loads[1].wait()
+
+    def pack_taps(o, carry):
+        to = lax.rem(me + o, n)
+        hsend[to], hsscale[to] = encode(taps_ref[:, lanes(to)])
+        return carry
+
+    lax.fori_loop(1, n, pack_taps, 0)
     loads[0].wait()
     for j in range(3):
         last = x_ref[j, rows - 16 :, :].astype(jnp.float32)
         tail[2 * j : 2 * j + 2, :] = last[14:16, :]
-    loads[1].wait()
     pl.semaphore_wait(barrier, n)
     after = pltpu.make_async_remote_copy(
         src_ref=tail,
@@ -252,8 +265,6 @@
     after.start()
 
     def send_taps(o, carry):
-        to = lax.rem(me + o, n)
-        hsend[to], hsscale[to] = encode(taps_ref[:, lanes(to)])
         for copy in taps_links(o):
             copy.start()
         return carry
@@ -284,11 +295,17 @@
     def send_gated(o, carry):
         to = lax.rem(me + o, n)
         gsend[to], gsscale[to] = encode(feature(to))
-        for copy in gated_links(o):
+        for copy in gated_links(o)[:2]:
             copy.start()
         return carry
 
     lax.fori_loop(1, n, send_gated, 0)
+
+    def send_rest(o, carry):
+        gated_links(o)[2].start()
+        return carry
+
+    lax.fori_loop(1, n, send_rest, 0)
     feature(me)
 
     def take_taps(o, carry):
@@ -301,7 +318,7 @@
     lax.fori_loop(1, n, take_taps, 0)
     for load in loads[3:8]:
         load.wait()
-    outer_forward(n, rows, outer, x, y)
+    outer_forward(n, 0, rows, outer, x, y)
 
     def spectrum(pair, carry):
         z[pair] = inner_forward(pair, rows, inner, turn, y)
@@ -310,15 +327,23 @@
     lax.fori_loop(0, (n + 2) // 2, spectrum, 0)
     x[me] = gated_ref[:, lanes(me)]
 
-    def take_gated(o, carry):
+    def take_low(o, carry):
         source = lax.rem(me - o + n, n)
-        for copy in gated_links(o):
+        for copy in gated_links(o)[:2]:
             copy.wait()
-        x[source] = decode(gcode[source], gscale[source])
-        return carry
-
-    lax.fori_loop(1, n, take_gated, 0)
-    outer_forward(n, rows, outer, x, y)
+        x[source, :half_rows, :] = decode(gcode[source, :half_rows, :], gscale[source])
+        return carry
+
+    def take_high(o, carry):
+        source = lax.rem(me - o + n, n)
+        gated_links(o)[2].wait()
+        x[source, half_rows:, :] = decode(gcode[source, half_rows:, :], gscale[source])
+        return carry
+
+    lax.fori_loop(1, n, take_low, 0)
+    outer_forward(n, 0, half_rows, outer, x, y)
+    lax.fori_loop(1, n, take_high, 0)
+    outer_forward(n, half_rows, rows, outer, x, y)
 
     def multiply(pair, carry):
         g = inner_forward(pair, rows, inner, turn, y)
@@ -348,11 +373,11 @@
         return carry
 
     for p in range(2):
-        lax.fori_loop(p * part // 32, (p + 1) * part // 32, blocks, 0)
+        lax.fori_loop(spans[p][0] // 32, spans[p][1] // 32, blocks, 0)
 
         def send_conv(o, carry, p=p):
             to = lax.rem(me + o, n)
-            at = pl.ds(p * part, part)
+            at = pl.ds(spans[p][0], spans[p][1] - spans[p][0])
             csend[to, at, :], csscale[p, to] = encode(x[to, at, :])
             for copy in conv_links(p, o):
                 copy.start()
@@ -364,45 +389,51 @@
         load.wait()
     mine[...] = jnp.zeros_like(mine)
 
-    def mix(p, d, conv):
-        at, cols = pl.ds(p * part, part), lanes(d)
+    def mix(at, d, conv):
+        cols = lanes(d)
         mixer = (conv + skip_ref[:, cols] * gated_ref[at, cols]) * one_ref[at, cols]
         mixed_ref[at, cols] = mixer.astype(jnp.bfloat16)
         both = stream_ref[at, cols].astype(jnp.float32) + mixer
         summed[at, cols] = both
         mine[at, :] += both * both
 
+    swaps = []
     for p in range(2):
-        mix(p, me, x[me, pl.ds(p * part, part), :])
-
-        def take_conv(o, carry, p=p):
+        at = pl.ds(spans[p][0], spans[p][1] - spans[p][0])
+        mix(at, me, x[me, at, :])
+
+        def take_conv(o, carry, p=p, at=at):
             source = lax.rem(me - o + n, n)
             for copy in conv_links(p, o):
                 copy.wait()
-            mix(p, source, decode(ccode[source, pl.ds(p * part, part), :], cscale[p, source]))
+            mix(at, source, decode(ccode[source, at, :], cscale[p, source]))
             return carry
 
         lax.fori_loop(1, n, take_conv, 0)
-
-    swap = pltpu.make_async_remote_copy(
-        src_ref=mine,
-        dst_ref=other,
-        send_sem=edge_sems.at[2],
-        recv_sem=edge_sems.at[3],
-        device_id={"chan": 1 - core},
-        device_id_type=MESH,
-    )
-    swap.start()
-    swap.wait()
-    power = jnp.sum(mine[...] + other[...], axis=1, keepdims=True)
-    factor = 1.0 / jnp.sqrt(power / D + 1e-05)
-
-    def norm(d, carry):
-        cols = lanes(d)
-        normed_ref[:, cols] = (summed[:, cols] * factor * gain_ref[:, cols]).astype(jnp.bfloat16)
-        return carry
-
-    lax.fori_loop(0, n, norm, 0)
+        swap = pltpu.make_async_remote_copy(
+            src_ref=mine.at[at],
+            dst_ref=other.at[at],
+            send_sem=edge_sems.at[2 + 2 * p],
+            recv_sem=edge_sems.at[3 + 2 * p],
+            device_id={"chan": 1 - core},
+            device_id_type=MESH,
+        )
+        swap.start()
+        swaps.append(swap)
+
+    for p in range(2):
+        at = pl.ds(spans[p][0], spans[p][1] - spans[p][0])
+        swaps[p].wait()
+        power = jnp.sum(mine[at, :] + other[at, :], axis=1, keepdims=True)
+        factor = 1.0 / jnp.sqrt(power / D + 1e-05)
+
+        def norm(d, carry, at=at, factor=factor):
+            cols = lanes(d)
+            normed = summed[at, cols] * factor * gain_ref[:, cols]
+            normed_ref[at, cols] = normed.astype(jnp.bfloat16)
+            return carry
+
+        lax.fori_loop(0, n, norm, 0)
 
 
 def fast(n, projected, short_weight, filter_taps, skip_gain, stream, norm_gain):
@@ -431,8 +462,8 @@
             pltpu.VMEM((rows, chans), f32),
             pltpu.VMEM((rows, 128), f32),
             pltpu.VMEM((rows, 128), f32),
-            pltpu.SemaphoreType.DMA((16, n)),
-            pltpu.SemaphoreType.DMA((4,)),
+            pltpu.SemaphoreType.DMA((18, n)),
+            pltpu.SemaphoreType.DMA((6,)),
             pltpu.SemaphoreType.DMA((len(operands),)),
         ],
         compiler_params=pltpu.CompilerParams(

time: 62.4 us -> 60.9 us (0.976)
  the two profiles are of different devices: /device:TPU:0 before, /device:TPU:13 now
where the time goes in v1:
time: 60.9 us; the launch traced here: 60 us
  Pallas kernels  55.6 us (91%)
  local copies, waits for them, and re-layouts  3.76 us (6%)
  between operations  0.64 us (1%)
    pallas_call x1, Pallas kernels, fast(): pl.pallas_call(functools.partial(kernel, n), out_shape=[jax.ShapeDtypeStr...  55.6 us
    unnamed x2, local copies, waits for them, and re-layouts  3.76 us

profile of v1, /device:TPU:13, one launch (start us, length us, event | category | flops | bytes accessed | tf_op | source)
XLA Modules:
  0.0 60.0 jit_solution(17370189950626890085)
XLA Ops:
  0.6 55.6 %mixer.1 = (bf16[128,2048]{1,0:T(8,128)(2,1)}, bf16[128,2048]{1,0:T(8,128)(2,1)}) custom-call(bf16[3,128,2048]{2,1,0:T(8,128)(2,1)} %bitcast.3, f32[3,3,2048]{2,1,0:T(4,128)} %w_hbm.1, f32[128,2048]{1,0:T(8,128)} %taps_hbm.1, f32[1,2048]{1,0:T(1,128)} %bitcast.4, bf16[128,2048]{1,0:T(8,128)(2,1)} %stream_hbm.1, f32[1,2048]{1,0:T(1,128)} %bitcast.5, ...), custom_call_target="tpu_custom_call" | custom-call | tf_op jit(solution)/shard_map/mixer/pallas_call | solution.py:448
  56.2 1.9 %copy.15 = bf16[128,2048]{1,0:T(8,128)(2,1)} copy(bf16[128,2048]{1,0:T(8,128)(2,1)} %get-tuple-element.4) | data formatting | bytes 1048576
  58.1 1.9 %copy.16 = bf16[128,2048]{1,0:T(8,128)(2,1)} copy(bf16[128,2048]{1,0:T(8,128)(2,1)} %get-tuple-element.5) | data formatting | bytes 1048576

commit v2 on v1

--- a/solution.py
+++ b/solution.py
@@ -163,7 +163,7 @@
             y[:, :, at, :] = u[:, 128 * half : 128 * half + 128].reshape(ks, 2, 16, 128)
         return carry
 
-    lax.fori_loop(begin // 32, end // 32, step, 0)
+    lax.fori_loop(begin // 32, end // 32, step, 0, unroll=True)
 
 
 def inner_forward(pair, rows, inner, turn, y):
@@ -359,7 +359,7 @@
             y[k, 1] = im * c + re * s
         return carry
 
-    lax.fori_loop(0, (n + 2) // 2, multiply, 0)
+    lax.fori_loop(0, (n + 2) // 2, multiply, 0, unroll=True)
 
     def blocks(j, carry):
         parts = []
@@ -373,7 +373,7 @@
         return carry
 
     for p in range(2):
-        lax.fori_loop(spans[p][0] // 32, spans[p][1] // 32, blocks, 0)
+        lax.fori_loop(spans[p][0] // 32, spans[p][1] // 32, blocks, 0, unroll=True)
 
         def send_conv(o, carry, p=p):
             to = lax.rem(me + o, n)

time: 60.9 us -> 56.6 us (0.929)
  Pallas kernels: 55.6 us -> 51.4 us
    pallas_call x1, Pallas kernels: 55.6 us -> 51.4 us  [fast(): pl.pallas_call(functools.partial(kernel, n), out_shape=[jax.ShapeDtypeStr...]
where the time goes in v2:
time: 56.6 us; the launch traced here: 55.8 us
  Pallas kernels  51.4 us (91%)
  local copies, waits for them, and re-layouts  3.76 us (7%)
  between operations  0.64 us (1%)
    pallas_call x1, Pallas kernels, fast(): pl.pallas_call(functools.partial(kernel, n), out_shape=[jax.ShapeDtypeStr...  51.4 us
    unnamed x2, local copies, waits for them, and re-layouts  3.76 us

profile of v2, /device:TPU:13, one launch (start us, length us, event | category | flops | bytes accessed | tf_op | source)
XLA Modules:
  0.0 55.8 jit_solution(5498045090673867877)
XLA Ops:
  0.6 51.4 %mixer.1 = (bf16[128,2048]{1,0:T(8,128)(2,1)}, bf16[128,2048]{1,0:T(8,128)(2,1)}) custom-call(bf16[3,128,2048]{2,1,0:T(8,128)(2,1)} %bitcast.3, f32[3,3,2048]{2,1,0:T(4,128)} %w_hbm.1, f32[128,2048]{1,0:T(8,128)} %taps_hbm.1, f32[1,2048]{1,0:T(1,128)} %bitcast.4, bf16[128,2048]{1,0:T(8,128)(2,1)} %stream_hbm.1, f32[1,2048]{1,0:T(1,128)} %bitcast.5, ...), custom_call_target="tpu_custom_call" | custom-call | tf_op jit(solution)/shard_map/mixer/pallas_call | solution.py:448
  52.0 1.9 %copy.15 = bf16[128,2048]{1,0:T(8,128)(2,1)} copy(bf16[128,2048]{1,0:T(8,128)(2,1)} %get-tuple-element.4) | data formatting | bytes 1048576
  53.9 1.9 %copy.16 = bf16[128,2048]{1,0:T(8,128)(2,1)} copy(bf16[128,2048]{1,0:T(8,128)(2,1)} %get-tuple-element.5) | data formatting | bytes 1048576
